TPU v7x, 32 devices: a whole 2x2x4 slice. The times are simulated.
32 devices in a mesh: groups: 2 (over y), gx: 16 (over z, x, core).
Axes of the slice: x: 2, y: 2, z: 4, core: 2. Of those that a mesh axis runs over, the one named last changes fastest.
Arguments:
- state: float32 [3, 32, 128, 256], P(None, ('groups', 'gx')), parts along dimension 1, may hold values from -4 to 4
- old_state: float32 [3, 32, 128, 256], P(None, ('groups', 'gx')), parts along dimension 1, may hold values from -4 to 4
- pore_volume: float32 [32, 128, 256], P(('groups', 'gx')), parts along dimension 0, may hold values from 0.5 to 2
- permeability: float32 [32, 128, 256], P(('groups', 'gx')), parts along dimension 0, may hold values from 0.2 to 2
- inverse_blocks: float32 [3, 3, 32, 128, 256], P(None, None, ('groups', 'gx')), parts along dimension 2, may hold values from -0.4 to 0.4
- perf_cells: int32 [2, 512], P(None, ('groups', 'gx')), parts along dimension 1, may hold values from -1 to 32767, as said below
- perf_wells: int32 [2, 512], P(None, ('groups', 'gx')), parts along dimension 1, may hold values from -1 to 15, as said below
- well_index: float32 [2, 512], P(None, ('groups', 'gx')), parts along dimension 1, may hold values from 0.5 to 2
- well_rates: float32 [512], P(('groups', 'gx')), parts along dimension 0, may hold values from -8 to 8
Outputs:
- new_state: float32 [3, 32, 128, 256], P(None, ('groups', 'gx')), parts along dimension 1
- residual: float32 [3, 32, 128, 256], P(None, ('groups', 'gx')), parts along dimension 1
- bottomhole: float32 [512], P(('groups', 'gx')), parts along dimension 0
There are 2 independent parts, one for each index of `groups`. A program takes and returns all parts, laid end to end along the dimension named above; each array names one. Nothing has to cross between parts.
Inputs may be any that keep to these rules, and one draw needn't show every extreme that they name: `perf_cells`: column s * 16 + d, row k: the cell that slot k from device s to owner d perforates, as a row-major index into device s's own cells, or -1 if the slot is empty. Every device fills all its slots to itself, and some device receives all slots filled from every device. `perf_wells`: column d * 16 + s, row k: the well of device d that slot k from device s belongs to, -1 exactly where the matching entry of perf_cells is -1. Every well has at least one live slot.
All inputs are finite; a program needn't handle non-finite values.
Results may differ from a plain program's by a relative error of at most 0.0003.
Values sent between devices are 32-bit elements; how exact they have to be, the bound alone decides.
A program may use at most 128 MiB of HBM per device.

v0:
```python
import jax
import jax.numpy as jnp
from jax import lax
from jax.sharding import PartitionSpec as P


def padded(block, sides, width):
    for axis, dim in sides:
        count = lax.axis_size(axis)
        forward = [(i, i + 1) for i in range(count - 1)]
        backward = [(target, source) for source, target in forward]
        low = lax.ppermute(
            lax.slice_in_dim(block, block.shape[dim] - width, None, axis=dim), axis, forward
        )
        high = lax.ppermute(lax.slice_in_dim(block, 0, width, axis=dim), axis, backward)
        block = jnp.concatenate([low, block, high], axis=dim)
    return block


def fractions(unknowns):
    first = jnp.exp(jnp.tanh(unknowns[1]))
    second = jnp.exp(jnp.tanh(unknowns[2]))
    total = 1.0 + first + second
    return jnp.stack([1.0 / total, first / total, second / total])


def accumulate(values):
    return values + 0.5 * jnp.tanh(values)


def shifted(array, step_x, step_y, step_z):
    size_x, size_y, size_z = (array.shape[-3], array.shape[-2], array.shape[-1])
    return array[
        ...,
        1 + step_x : size_x - 1 + step_x,
        1 + step_y : size_y - 1 + step_y,
        1 + step_z : size_z - 1 + step_z,
    ]


def flux_sum(ext_u, ext_k):
    frac = fractions(ext_u)
    press = ext_u[0]
    k_center = shifted(ext_k, 0, 0, 0)
    p_center = shifted(press, 0, 0, 0)
    f_center = shifted(frac, 0, 0, 0)
    total = jnp.zeros_like(f_center)
    for step_x, step_y, step_z in (
        (1, 0, 0),
        (-1, 0, 0),
        (0, 1, 0),
        (0, -1, 0),
        (0, 0, 1),
        (0, 0, -1),
    ):
        k_near = shifted(ext_k, step_x, step_y, step_z)
        p_near = shifted(press, step_x, step_y, step_z)
        f_near = shifted(frac, step_x, step_y, step_z)
        trans = 2.0 * k_center * k_near / (k_center + k_near)
        total = total + (trans * (p_center - p_near))[None] * 0.5 * (f_center + f_near)
    return total


def cell_part(ext_u, ext_k, pore, old):
    center = ext_u[:, 1:-1, 1:-1, 1:-1]
    return pore[None] * (accumulate(center) - accumulate(old)) + flux_sum(ext_u, ext_k)


def owner(blocks, wells, index_w, rates):
    valid = wells >= 0
    weight = jnp.where(valid, index_w, 0.0)
    count = rates.shape[0]
    onehot = (wells[None] == jnp.arange(count, dtype=jnp.int32)[:, None, None]).astype(rates.dtype)
    weight_sum = jnp.sum(onehot * weight[None], axis=(1, 2))
    press_sum = jnp.sum(onehot * (weight * blocks[0])[None], axis=(1, 2))
    bottom = (rates + press_sum) / weight_sum
    at_slot = jnp.sum(onehot * bottom[:, None, None], axis=0)
    flow = weight * (at_slot - blocks[0])
    return (flow[None] * fractions(blocks), bottom)


def apply_blocks(blocks, values):
    return jnp.sum(blocks * values[None], axis=1)


def deliver(blocks):
    return lax.all_to_all(blocks, "gx", split_axis=2, concat_axis=2, tiled=True)


def collect(sources):
    return lax.all_to_all(sources, "gx", split_axis=2, concat_axis=2, tiled=True)


def pad_sides(extended):
    return jnp.pad(extended, ((0, 0), (0, 0), (1, 1), (1, 1)))


def shards(
    state,
    old_state,
    pore_volume,
    permeability,
    inverse_blocks,
    perf_cells,
    perf_wells,
    well_index,
    well_rates,
):
    cells = state.shape[1] * state.shape[2] * state.shape[3]
    stacked = jnp.concatenate([state, permeability[None]], 0)
    extended = pad_sides(padded(stacked, (("gx", 1),), 1))
    ext_u = extended[:3]
    ext_k = extended[3]
    cell = cell_part(ext_u, ext_k, pore_volume, old_state)
    safe = jnp.maximum(perf_cells, 0)
    mask = (perf_cells >= 0).astype(state.dtype)

    def spread(values):
        placed = jnp.zeros((3, cells), state.dtype).at[:, safe].add(values * mask[None])
        return placed.reshape(state.shape)

    def well_part(blocks):
        return owner(blocks, perf_wells, well_index, well_rates)

    received = deliver(state.reshape(3, cells)[:, safe])
    sources, bottomhole = well_part(received)
    residual = cell - spread(collect(sources))
    correction = apply_blocks(inverse_blocks, -residual)
    ext_v = pad_sides(padded(correction, (("gx", 1),), 1))
    cell_tangent = jax.jvp(
        lambda values: cell_part(values, ext_k, pore_volume, old_state), (ext_u,), (ext_v,)
    )[1]
    received_v = deliver(correction.reshape(3, cells)[:, safe])
    source_tangent = jax.jvp(well_part, (received,), (received_v,))[1][0]
    tangent = cell_tangent - spread(collect(source_tangent))
    correction = correction + apply_blocks(inverse_blocks, -residual - tangent)
    return (state + correction, residual, bottomhole)


def solution(mesh):
    return jax.shard_map(
        shards,
        mesh=mesh,
        in_specs=(
            P(None, ("groups", "gx"), None, None),
            P(None, ("groups", "gx"), None, None),
            P(("groups", "gx"), None, None),
            P(("groups", "gx"), None, None),
            P(None, None, ("groups", "gx"), None, None),
            P(None, ("groups", "gx")),
            P(None, ("groups", "gx")),
            P(None, ("groups", "gx")),
            P(("groups", "gx")),
        ),
        out_specs=(
            P(None, ("groups", "gx"), None, None),
            P(None, ("groups", "gx"), None, None),
            P(("groups", "gx")),
        ),
        check_vma=False,
    )
```

profile of v0, /device:TPU:0, one launch (start us, length us, event | category | flops | bytes accessed | tf_op | source)
XLA Modules:
  0.0 149.5 jit_solution(4410542287746046466)
XLA Ops:
  1.5 9.6 %copy.88 = f32[3,1,128,256]{0,3,2,1:T(8,128)} copy(f32[3,1,128,256]{3,2,1,0:T(8,128)} %param.9) | data formatting | bytes 786432 | tf_op args[0]
  11.1 6.3 %gather_fusion = f32[32,3]{1,0:T(8,128)S(1)} fusion(f32[3,32768]{0,1:T(8,128)} %bitcast.76, s32[1024]{0:T(1024)S(1)} %pad_clamp_fusion), kind=kCustom, calls=%fused_computation | custom fusion | bytes 896 | tf_op jit(solution)/shard_map/gather | solution.py:125
  18.1 7.4 %all-to-all-start = ((f32[3,2,16]{0,1,2:T(2,128)}), f32[3,2,16]{0,1,2:T(2,128)S(1)}, u32[]{:S(2)}, u32[]{:S(2)}) async-start(f32[3,2,16]{0,1,2:T(2,128)} %bitcast.72), calls=%async_computation | async-start | bytes 32768 | tf_op jit(solution)/shard_map/all_to_all | solution.py:87
  25.5 2.3 %collective-permute-start = (f32[4,1,128,256]{3,2,1,0:T(8,128)S(1)}, f32[4,1,128,256]{3,2,1,0:T(8,128)S(1)}, u32[]{:S(2)}, u32[]{:S(2)}) collective-permute-start(f32[4,1,128,256]{3,2,1,0:T(8,128)S(1)} %pad_maximum_fusion.2), channel_id=1, source_target_pairs={{0,1},{1,2},{2,3},{3,4},{4,5},{5,6},{6,7},{7,8},{8,9},{9,10},{10,1... | collective-permute-start | bytes 1572872 | tf_op jit(solution)/shard_map/ppermute | solution.py:12
  27.9 1.3 collective-permute-start.1
  29.2 2.8 %all-to-all-done = f32[3,2,16]{0,1,2:T(2,128)S(1)} async-done(((f32[3,2,16]{0,1,2:T(2,128)}), f32[3,2,16]{0,1,2:T(2,128)S(1)}, u32[]{:S(2)}, u32[]{:S(2)}) %all-to-all-start) | async-done | bytes 416 | tf_op jit(solution)/shard_map/all_to_all | solution.py:87
  34.7 5.2 %all-to-all-start.1 = ((f32[3,2,16]{0,1,2:T(2,128)}), f32[3,2,16]{0,1,2:T(2,128)S(1)}, u32[]{:S(2)}, u32[]{:S(2)}) async-start(f32[3,2,16]{0,1,2:T(2,128)} %copy.94), calls=%async_computation.1 | async-start | bytes 32768 | tf_op jit(solution)/shard_map/all_to_all | solution.py:91
  40.0 6.4 %all-to-all-done.1 = f32[3,2,16]{0,1,2:T(2,128)S(1)} async-done(((f32[3,2,16]{0,1,2:T(2,128)}), f32[3,2,16]{0,1,2:T(2,128)S(1)}, u32[]{:S(2)}, u32[]{:S(2)}) %all-to-all-start.1) | async-done | bytes 416 | tf_op jit(solution)/shard_map/all_to_all | solution.py:91
  46.5 7.5 %scatter_custom_fusion = f32[3,32768]{0,1:T(8,128)} fusion(s32[32]{0:T(128)S(1)} %reshape.209, f32[32,3]{1,0:T(8,128)S(1)} %bitcast.88, f32[]{:T(128)} %constant.8.clone.1), kind=kCustom, calls=%fused_computation.6 | custom fusion | flops 96 | bytes 393220 | tf_op jit(solution)/shard_map/scatter-add | solution.py:119
  54.0 10.0 %copy.98 = f32[3,1,128,256]{3,2,1,0:T(8,128)S(1)} copy(f32[3,1,128,256]{0,3,2,1:T(8,128)} %bitcast.74) | data formatting | bytes 786432 | tf_op jit(solution)/shard_map/reshape | solution.py:120
  68.0 1.5 negate_bitcast_fusion
  69.6 8.6 %copy.99 = f32[3,128,256]{0,2,1:T(8,128)} copy(f32[3,128,256]{2,1,0:T(8,128)S(1)} %multiply_reduce_fusion.1) | data formatting | bytes 786432 | tf_op jit(solution)/shard_map/reduce_sum | solution.py:83
  78.3 7.1 %gather_fusion.1 = f32[32,3]{1,0:T(8,128)} fusion(f32[3,32768]{0,1:T(8,128)} %bitcast.75, s32[1024]{0:T(1024)} %copy-done.25), kind=kCustom, calls=%fused_computation.1 | custom fusion | bytes 896 | tf_op jit(solution)/shard_map/gather | solution.py:133
  85.3 1.3 copy.123
  86.6 4.1 %all-to-all-start.2 = ((f32[3,2,16]{0,1,2:T(2,128)}), f32[3,2,16]{0,1,2:T(2,128)}, u32[]{:S(2)}, u32[]{:S(2)}) async-start(f32[3,2,16]{0,1,2:T(2,128)} %bitcast.84), calls=%async_computation.2 | async-start | bytes 32768 | tf_op jit(solution)/shard_map/all_to_all | solution.py:87
  90.8 2.9 %collective-permute-start.2 = (f32[3,1,128,256]{3,2,1,0:T(8,128)S(1)}, f32[3,1,128,256]{3,2,1,0:T(8,128)}, u32[]{:S(2)}, u32[]{:S(2)}) collective-permute-start(f32[3,1,128,256]{3,2,1,0:T(8,128)S(1)} %bitcast.77), channel_id=1, source_target_pairs={{0,1},{1,2},{2,3},{3,4},{4,5},{5,6},{6,7},{7,8},{8,9},{9,10},{10,1... | collective-permute-start | bytes 1179656 | tf_op jit(solution)/shard_map/ppermute | solution.py:12
  93.6 1.3 collective-permute-start.3
  94.9 2.3 %all-to-all-done.2 = f32[3,2,16]{0,1,2:T(2,128)} async-done(((f32[3,2,16]{0,1,2:T(2,128)}), f32[3,2,16]{0,1,2:T(2,128)}, u32[]{:S(2)}, u32[]{:S(2)}) %all-to-all-start.2) | async-done | bytes 416 | tf_op jit(solution)/shard_map/all_to_all | solution.py:87
  97.3 1.5 %fusion.81 = (f32[1,2,16]{0,1,2:T(2,128)}, f32[1,2,16]{0,1,2:T(2,128)}, f32[1,2,16]{0,1,2:T(2,128)}) fusion(f32[3,2,16]{0,1,2:T(2,128)} %all-to-all-done.2), kind=kLoop, calls=%fused_computation.181 | loop fusion | bytes 768 | tf_op jit(solution)/shard_map/jvp()/slice | solution.py:75
  98.8 1.4 copy.102
  103.0 1.2 fusion.76
  104.3 1.4 copy.119
  105.6 1.4 copy.120
  107.7 1.3 fusion.75
  109.0 1.4 copy.105
  110.4 11.5 %all_to_all.20 = f32[3,2,16]{0,1,2:T(2,128)S(1)} all-to-all(f32[3,2,16]{0,1,2:T(2,128)} %copy.105), channel_id=1, replica_groups=mesh['groups'=2,'gx'=16] {'gx'}, dimensions={2} | all-to-all | bytes 768 | tf_op jit(solution)/shard_map/all_to_all | solution.py:91
  123.3 7.7 %scatter_custom_fusion.1 = f32[3,32768]{0,1:T(8,128)} fusion(s32[32]{0:T(128)} %copy-done.35, f32[32,3]{1,0:T(8,128)} %bitcast.87, f32[]{:T(128)} %constant.8.clone.1), kind=kCustom, calls=%fused_computation.4 | custom fusion | flops 96 | bytes 393728 | tf_op jit(solution)/shard_map/scatter-add | solution.py:119
  131.0 10.7 %copy.108 = f32[3,1,128,256]{3,2,1,0:T(8,128)} copy(f32[3,1,128,256]{0,3,2,1:T(8,128)} %bitcast.73) | data formatting | bytes 786432 | tf_op jit(solution)/shard_map/reshape | solution.py:120
  141.6 1.9 %select_maximum_fusion.3 = f32[3,3,130,258]{3,2,1,0:T(8,128)S(1)} fusion(f32[3,1,128,256]{3,2,1,0:T(8,128)} %collective-permute-done.3, f32[3,1,128,256]{3,2,1,0:T(8,128)S(1)} %bitcast.79, f32[3,1,128,256]{3,2,1,0:T(8,128)} %collective-permute-done.2), kind=kLoop, calls=%fused_computation.22 | loop fusion | flops 4527900 | bytes 2387088 | tf_op jit(solution)/shard_map/concatenate | solution.py:16
  143.6 1.8 %fusion.14 = (f32[1,3,130,258]{3,2,1,0:T(8,128)S(1)}, f32[1,3,130,258]{3,2,1,0:T(8,128)S(1)}, f32[1,3,130,258]{3,2,1,0:T(8,128)S(1)}, f32[3,130,258]{2,1,0:T(8,128)S(1)}) fusion(f32[1,3,130,258]{3,2,1,0:T(8,128)} %copy-done.3, f32[4,3,130,258]{3,2,1,0:T(8,128)S(1)} %copy-done.1, f32[3,3,130,258]{3,2,1,0:T(8,128)S(1)} %select_maximum_fusion.3), kind=kLoop, calls=%fused_computation.48 | loop fusion | flops 2314260 | bytes 4024800 | tf_op jit(solution)/shard_map/jvp()/mul | solution.py:24
  147.1 1.4 fusion.21
  148.6 0.8 fusion.36
  (118 shorter events, 15.2 us)
Async XLA Ops:
  1.4 45.1 %copy-start.35 = (s32[32]{0:T(128)}, s32[32]{0:T(128)S(1)}, u32[]{:S(2)}) copy-start(s32[32]{0:T(128)S(1)} %reshape.209) | copy-start | bytes 388
  1.4 9.7 %copy-start.25 = (s32[1024]{0:T(1024)}, s32[1024]{0:T(1024)S(1)}, u32[]{:S(2)}) copy-start(s32[1024]{0:T(1024)S(1)} %pad_clamp_fusion) | copy-start | bytes 12292
  1.4 24.0 %copy-start.2 = (f32[3,1,128,256]{3,2,1,0:T(8,128)S(1)}, f32[3,1,128,256]{3,2,1,0:T(8,128)}, u32[]{:S(2)}) copy-start(f32[3,1,128,256]{3,2,1,0:T(8,128)} %param.9) | copy-start | bytes 1179652
  1.4 24.0 %copy-start.18 = (f32[1,128,256]{2,1,0:T(8,128)S(1)}, f32[1,128,256]{2,1,0:T(8,128)}, u32[]{:S(2)}) copy-start(f32[1,128,256]{2,1,0:T(8,128)} %param.12) | copy-start | bytes 393220
  1.4 30.7 %copy-start.21 = (s32[2,16]{1,0:T(2,128)S(1)}, s32[2,16]{1,0:T(2,128)}, u32[]{:S(2)}) copy-start(s32[2,16]{1,0:T(2,128)} %param.15) | copy-start | bytes 388
  1.4 30.7 %copy-start.34 = (f32[2,16]{1,0:T(2,128)S(1)}, f32[2,16]{1,0:T(2,128)}, u32[]{:S(2)}) copy-start(f32[2,16]{1,0:T(2,128)} %param.16) | copy-start | bytes 388
  1.5 30.8 %copy-start.36 = (f32[16]{0:T(128)S(1)}, f32[16]{0:T(128)}, u32[]{:S(2)}) copy-start(f32[16]{0:T(128)} %param.17) | copy-start | bytes 196
  1.5 38.4 %copy-start.31 = (s32[2,16]{1,0:T(2,128)S(1)}, s32[2,16]{1,0:T(2,128)}, u32[]{:S(2)}) copy-start(s32[2,16]{1,0:T(2,128)} %param.14) | copy-start | bytes 388
  18.1 13.9 %all-to-all-start = ((f32[3,2,16]{0,1,2:T(2,128)}), f32[3,2,16]{0,1,2:T(2,128)S(1)}, u32[]{:S(2)}, u32[]{:S(2)}) async-start(f32[3,2,16]{0,1,2:T(2,128)} %bitcast.72), calls=%async_computation | async-start | bytes 32768 | tf_op jit(solution)/shard_map/all_to_all | solution.py:87
  25.5 38.4 %collective-permute-start = (f32[4,1,128,256]{3,2,1,0:T(8,128)S(1)}, f32[4,1,128,256]{3,2,1,0:T(8,128)S(1)}, u32[]{:S(2)}, u32[]{:S(2)}) collective-permute-start(f32[4,1,128,256]{3,2,1,0:T(8,128)S(1)} %pad_maximum_fusion.2), channel_id=1, source_target_pairs={{0,1},{1,2},{2,3},{3,4},{4,5},{5,6},{6,7},{7,8},{8,9},{9,10},{10,1... | collective-permute-start | bytes 1572872 | tf_op jit(solution)/shard_map/ppermute | solution.py:12
  27.9 36.1 %collective-permute-start.1 = (f32[4,1,128,256]{3,2,1,0:T(8,128)S(1)}, f32[4,1,128,256]{3,2,1,0:T(8,128)S(1)}, u32[]{:S(2)}, u32[]{:S(2)}) collective-permute-start(f32[4,1,128,256]{3,2,1,0:T(8,128)S(1)} %pad_maximum_fusion.2), channel_id=1, source_target_pairs={{1,0},{2,1},{3,2},{4,3},{5,4},{6,5},{7,6},{8,7},{9,8},{10,9},{11,1... | collective-permute-start | bytes 1572872 | tf_op jit(solution)/shard_map/ppermute | solution.py:15
  32.2 7.7 %copy-start.22 = (f32[2,16]{1,0:T(2,128)}, f32[2,16]{1,0:T(2,128)S(1)}, u32[]{:S(2)}) copy-start(f32[2,16]{1,0:T(2,128)S(1)} %get-tuple-element.12) | copy-start | bytes 388
  32.9 21.1 %copy-start.28 = (f32[2,16]{1,0:T(2,128)}, f32[2,16]{1,0:T(2,128)S(1)}, u32[]{:S(2)}) copy-start(f32[2,16]{1,0:T(2,128)S(1)} %fusion.77) | copy-start | bytes 388
  33.0 6.9 %copy-start.23 = (f32[1,2,16]{2,1,0:T(2,128)}, f32[1,2,16]{2,1,0:T(2,128)S(1)}, u32[]{:S(2)}) copy-start(f32[1,2,16]{2,1,0:T(2,128)S(1)} %copy.117) | copy-start | bytes 388
  33.4 1.3 copy-start.24
  33.4 6.5 %copy-start.29 = (f32[1,2,16]{2,1,0:T(2,128)}, f32[1,2,16]{2,1,0:T(2,128)S(1)}, u32[]{:S(2)}) copy-start(f32[1,2,16]{2,1,0:T(2,128)S(1)} %get-tuple-element.9) | copy-start | bytes 388
  33.5 1.2 copy-start.26
  34.7 11.7 %all-to-all-start.1 = ((f32[3,2,16]{0,1,2:T(2,128)}), f32[3,2,16]{0,1,2:T(2,128)S(1)}, u32[]{:S(2)}, u32[]{:S(2)}) async-start(f32[3,2,16]{0,1,2:T(2,128)} %copy.94), calls=%async_computation.1 | async-start | bytes 32768 | tf_op jit(solution)/shard_map/all_to_all | solution.py:91
  40.0 14.0 %copy-start.20 = (f32[2,16]{0,1:T(8,128)}, f32[2,16]{0,1:T(8,128)S(1)}, u32[]{:S(2)}) copy-start(f32[2,16]{0,1:T(8,128)S(1)} %copy.95) | copy-start | bytes 388
  64.7 1.5 copy-start
  66.8 2.7 %copy-start.8 = (f32[128,256]{1,0:T(8,128)}, f32[128,256]{1,0:T(8,128)S(1)}, u32[]{:S(2)}) copy-start(f32[128,256]{1,0:T(8,128)S(1)} %get-tuple-element.29) | copy-start | bytes 393220
  66.8 2.7 %copy-start.10 = (f32[128,256]{1,0:T(8,128)}, f32[128,256]{1,0:T(8,128)S(1)}, u32[]{:S(2)}) copy-start(f32[128,256]{1,0:T(8,128)S(1)} %get-tuple-element.30) | copy-start | bytes 393220
  67.1 2.4 %copy-start.12 = (f32[128,256]{1,0:T(8,128)}, f32[128,256]{1,0:T(8,128)S(1)}, u32[]{:S(2)}) copy-start(f32[128,256]{1,0:T(8,128)S(1)} %get-tuple-element.31) | copy-start | bytes 393220
  67.1 2.4 %copy-start.14 = (f32[128,256]{1,0:T(8,128)}, f32[128,256]{1,0:T(8,128)S(1)}, u32[]{:S(2)}) copy-start(f32[128,256]{1,0:T(8,128)S(1)} %get-tuple-element.32) | copy-start | bytes 393220
  68.0 1.5 copy-start.4
  86.6 10.6 %all-to-all-start.2 = ((f32[3,2,16]{0,1,2:T(2,128)}), f32[3,2,16]{0,1,2:T(2,128)}, u32[]{:S(2)}, u32[]{:S(2)}) async-start(f32[3,2,16]{0,1,2:T(2,128)} %bitcast.84), calls=%async_computation.2 | async-start | bytes 32768 | tf_op jit(solution)/shard_map/all_to_all | solution.py:87
  90.8 50.8 %collective-permute-start.2 = (f32[3,1,128,256]{3,2,1,0:T(8,128)S(1)}, f32[3,1,128,256]{3,2,1,0:T(8,128)}, u32[]{:S(2)}, u32[]{:S(2)}) collective-permute-start(f32[3,1,128,256]{3,2,1,0:T(8,128)S(1)} %bitcast.77), channel_id=1, source_target_pairs={{0,1},{1,2},{2,3},{3,4},{4,5},{5,6},{6,7},{7,8},{8,9},{9,10},{10,1... | collective-permute-start | bytes 1179656 | tf_op jit(solution)/shard_map/ppermute | solution.py:12
  93.6 48.0 %collective-permute-start.3 = (f32[3,1,128,256]{3,2,1,0:T(8,128)S(1)}, f32[3,1,128,256]{3,2,1,0:T(8,128)}, u32[]{:S(2)}, u32[]{:S(2)}) collective-permute-start(f32[3,1,128,256]{3,2,1,0:T(8,128)S(1)} %bitcast.78), channel_id=1, source_target_pairs={{1,0},{2,1},{3,2},{4,3},{5,4},{6,5},{7,6},{8,7},{9,8},{10,9},{11,1... | collective-permute-start | bytes 1179656 | tf_op jit(solution)/shard_map/ppermute | solution.py:15
  141.6 1.9 %copy-start.1 = (f32[4,3,130,258]{3,2,1,0:T(8,128)S(1)}, f32[4,3,130,258]{3,2,1,0:T(8,128)}, u32[]{:S(2)}) copy-start(f32[4,3,130,258]{3,2,1,0:T(8,128)} %copy-done) | copy-start | bytes 4829764
  145.8 1.2 copy-start.15
  145.8 1.2 copy-start.17
  147.1 1.4 copy-start.5
  (12 other events, 11.7 us)
where the time goes:
time: 151 us; the launch traced here: 149 us
  local copies, waits for them, and re-layouts  67 us (44%)
  other arithmetic  33.9 us (22%)
  starting transfers between devices  24.4 us (16%)
  waiting for transfers between devices  11.5 us (8%)
  blocking collectives  11.5 us (8%)
    reshape x2, local copies, waits for them, and re-layouts, spread(): return placed.reshape(state.shape)  20.6 us
    unnamed x79, local copies, waits for them, and re-layouts  16.5 us
    scatter-add x2, other arithmetic, spread(): jnp.zeros((3, cells), state.dtype).at[:, safe].add(values * mask[None])  15.2 us
    all_to_all x1, blocking collectives, collect(): lax.all_to_all(sources, 'gx', split_axis=2, concat_axis=2, tiled=True)  11.5 us
    all_to_all x2, starting transfers between devices, deliver(): return lax.all_to_all(blocks, 'gx', split_axis=2, concat_axis=2, tiled=True)  11.5 us
    reduce_sum x1, local copies, waits for them, and re-layouts, apply_blocks(): return jnp.sum(blocks * values[None], axis=1)  8.63 us
    gather x2, local copies, waits for them, and re-layouts, shards(): received_v = deliver(correction.reshape(3, cells)[:, safe])  8.38 us
    gather x2, local copies, waits for them, and re-layouts, shards(): received = deliver(state.reshape(3, cells)[:, safe])  6.96 us
  transfers between devices with their start and end apart: 7, of which 3 were waited for; matrix products, arithmetic and copies ran while one was open for 35% of the time, Pallas kernels for 0%

commit v1 on v0

v1 whole, which is shorter than its diff:
```python
import functools

import jax
import jax.numpy as jnp
from jax import lax
from jax.experimental import pallas as pl
from jax.experimental.pallas import tpu as pltpu
from jax.sharding import PartitionSpec as P

CHUNKS = 4
MESH = pl.DeviceIdType.MESH
EXACT = lax.Precision.HIGHEST


def contract(left, right, left_dim, right_dim):
    return lax.dot_general(
        left,
        right,
        (((left_dim,), (right_dim,)), ((), ())),
        precision=EXACT,
        preferred_element_type=jnp.float32,
    )


def fractions(first, second):
    e1 = jnp.exp(jnp.tanh(first))
    e2 = jnp.exp(jnp.tanh(second))
    inverse = 1.0 / (1.0 + e1 + e2)
    return e1 * inverse, e2 * inverse


def transmissibility(k_a, k_b):
    return 2.0 * k_a * k_b / (k_a + k_b)


def kernel(
    n,
    state_hbm,
    old_hbm,
    pore_hbm,
    perm_hbm,
    inv_hbm,
    cells_ref,
    wells_ref,
    index_ref,
    rates_ref,
    new_ref,
    res_ref,
    bottom_ref,
    u,
    old,
    pore,
    perm,
    inv,
    halo_u,
    halo_k,
    halo_d,
    send_d,
    corr,
    frac,
    slope,
    accum,
    face,
    edge,
    part,
    source,
    message,
    inbox,
    message_d,
    inbox_d,
    load_sem,
    well_send,
    well_recv,
    welld_send,
    welld_recv,
    bulk_send,
    bulk_recv,
    bulkd_send,
    bulkd_recv,
):
    me = lax.axis_index("gx")
    ny, nz = perm.shape
    rows = ny // CHUNKS
    caps = cells_ref.shape[0]
    nwell = rates_ref.shape[1]

    loads = [
        pltpu.make_async_copy(state_hbm.at[:, 0], u, load_sem.at[0]),
        pltpu.make_async_copy(perm_hbm.at[0], perm, load_sem.at[1]),
        pltpu.make_async_copy(old_hbm.at[:, 0], old, load_sem.at[2]),
        pltpu.make_async_copy(pore_hbm.at[0], pore, load_sem.at[3]),
        pltpu.make_async_copy(inv_hbm.at[:, :, 0], inv, load_sem.at[4]),
    ]
    for load in loads:
        load.start()

    barrier = pltpu.get_barrier_semaphore()

    @pl.loop(1, n)
    def _(step):
        pl.semaphore_signal(
            barrier, inc=1, device_id={"gx": lax.rem(me + step, n)}, device_id_type=MESH
        )

    cells = cells_ref[...]
    cell_y = cells // nz
    cell_z = cells - cell_y * nz
    at_y = [
        (lax.broadcasted_iota(jnp.int32, (ny, n), 0) == cell_y[k : k + 1]).astype(jnp.float32)
        for k in range(caps)
    ]
    at_z = [
        (lax.broadcasted_iota(jnp.int32, (nz, n), 0) == cell_z[k : k + 1]).astype(jnp.float32)
        for k in range(caps)
    ]

    def pick(plane, k):
        return jnp.sum(contract(plane, at_z[k], 1, 0) * at_y[k], axis=0, keepdims=True)

    wells = wells_ref[...]
    weights = jnp.where(wells >= 0, index_ref[...], 0.0)
    message[...] = jnp.zeros_like(message)
    message[caps : 2 * caps, :n] = weights
    message[2 * caps : 3 * caps, :n] = wells.astype(jnp.float32)
    message[3 * caps : 3 * caps + 1, :nwell] = rates_ref[...]
    loads[0].wait()
    for k in range(caps):
        message[k : k + 1, :n] = pick(u[0], k)
    inbox[me] = message[...]
    loads[1].wait()

    pl.semaphore_wait(barrier, n - 1)

    def well_copy(source_ref, box, sends, receives, step):
        target = lax.rem(me + step, n)
        return pltpu.make_async_remote_copy(
            src_ref=source_ref,
            dst_ref=box.at[me],
            send_sem=sends.at[target],
            recv_sem=receives.at[me],
            device_id={"gx": target},
            device_id_type=MESH,
        )

    def well_arrival(source_ref, box, sends, receives, step):
        origin = lax.rem(me + step, n)
        return pltpu.make_async_remote_copy(
            src_ref=source_ref,
            dst_ref=box.at[origin],
            send_sem=sends.at[origin],
            recv_sem=receives.at[origin],
            device_id={"gx": origin},
            device_id_type=MESH,
        )

    @pl.loop(1, n)
    def _(step):
        well_copy(message, inbox, well_send, well_recv, step).start()

    near = (me > 0, me < n - 1)
    place = (me - 1, me + 1)

    def bulk_copies(side, c):
        span = pl.ds(c * rows, rows)
        lands = 1 - side
        pairs = (
            (u.at[:, span], halo_u.at[lands, :, span]),
            (perm.at[span], halo_k.at[lands, span]),
        )
        return [
            pltpu.make_async_remote_copy(
                src_ref=src,
                dst_ref=dst,
                send_sem=bulk_send.at[side, c, i],
                recv_sem=bulk_recv.at[lands, c, i],
                device_id={"gx": place[side]},
                device_id_type=MESH,
            )
            for i, (src, dst) in enumerate(pairs)
        ]

    def tangent_copy(side, c):
        span = pl.ds(c * rows, rows)
        lands = 1 - side
        return pltpu.make_async_remote_copy(
            src_ref=send_d.at[:, span],
            dst_ref=halo_d.at[lands, :, span],
            send_sem=bulkd_send.at[side, c],
            recv_sem=bulkd_recv.at[lands, c],
            device_id={"gx": place[side]},
            device_id_type=MESH,
        )

    for c in range(CHUNKS):
        for side in range(2):

            @pl.when(near[side])
            def _(side=side, c=c):
                for copy in bulk_copies(side, c):
                    copy.start()

    for side in range(2):

        @pl.when(jnp.logical_not(near[side]))
        def _(side=side):
            halo_u[side] = jnp.zeros_like(halo_u[side])
            halo_k[side] = jnp.zeros_like(halo_k[side])
            halo_d[side] = jnp.zeros_like(halo_d[side])

    for load in loads[2:4]:
        load.wait()
    p, k_here = u[0], perm[...]
    f1, f2 = fractions(u[1], u[2])
    frac[0] = f1
    frac[1] = f2
    for i in range(3):
        tan = jnp.tanh(u[i])
        rise = 1.0 - tan * tan
        part[i] = pore[...] * (u[i] + 0.5 * tan - (old[i] + 0.5 * jnp.tanh(old[i])))
        accum[i] = pore[...] * (1.0 + 0.5 * rise)
        if i:
            slope[i - 1] = rise

    for axis, size in ((0, ny), (1, nz)):
        last = lax.broadcasted_iota(jnp.int32, (ny, nz), axis) == size - 1
        trans = transmissibility(k_here, pltpu.roll(k_here, size - 1, axis))
        trans = jnp.where(last, 0.0, trans)
        total = trans * (p - pltpu.roll(p, size - 1, axis))
        s1 = 0.5 * (f1 + pltpu.roll(f1, size - 1, axis))
        s2 = 0.5 * (f2 + pltpu.roll(f2, size - 1, axis))
        face[axis, 0] = trans
        face[axis, 1] = 0.5 * total
        face[axis, 2] = s1
        face[axis, 3] = s2
        flow1, flow2 = total * s1, total * s2
        flow0 = total - flow1 - flow2
        for i, flow in enumerate((flow0, flow1, flow2)):
            part[i] += flow - pltpu.roll(flow, 1, axis)

    @pl.loop(1, n)
    def _(step):
        well_arrival(message, inbox, well_send, well_recv, step).wait_recv()

    lane = lax.broadcasted_iota(jnp.int32, (n, n), 1)
    eye = (lax.broadcasted_iota(jnp.int32, (n, n), 0) == lane).astype(jnp.float32)
    mine = lane == me

    def turned(values):
        return contract(eye, values, 1, 1)

    def own(values):
        return jnp.sum(jnp.where(mine, values, 0.0), axis=1, keepdims=True)

    press = [turned(inbox[:, k, :n]) for k in range(caps)]
    weight = [inbox[:, caps + k, :n] for k in range(caps)]
    well = [inbox[:, 2 * caps + k, :n] for k in range(caps)]
    rates = inbox[:, 3 * caps, :nwell]
    well_lane = lax.broadcasted_iota(jnp.int32, (n, nwell), 1).astype(jnp.float32)
    my_weight, shares, flows = [], [], []
    for k in range(caps):
        my_well = own(well[k])
        live = my_well >= 0.0
        taken = [jnp.where(well[j] == my_well, weight[j], 0.0) for j in range(caps)]
        whole = sum(jnp.sum(t, axis=1, keepdims=True) for t in taken)
        inverse = 1.0 / jnp.where(live, whole, 1.0)
        rate = jnp.sum(jnp.where(well_lane == my_well, rates, 0.0), axis=1, keepdims=True)
        lift = sum(jnp.sum(t * b, axis=1, keepdims=True) for t, b in zip(taken, press))
        pull = jnp.where(live, own(weight[k]), 0.0)
        flows.append(pull * ((rate + lift) * inverse - own(press[k])))
        my_weight.append(pull)
        shares.append([t * inverse for t in taken])

    def spread(columns):
        plane = None
        for k in range(caps):
            line = jnp.sum(columns[k] * eye, axis=0, keepdims=True)
            term = contract(at_y[k] * line, at_z[k], 1, 1)
            plane = term if plane is None else plane + term
        return plane

    source[0] = spread(flows)

    row_mine = lax.broadcasted_iota(jnp.int32, (n, n), 0) == me
    own_well = lax.broadcasted_iota(jnp.int32, (nwell, n), 0)
    w_sum = jnp.zeros((nwell, 1), jnp.float32)
    p_sum = jnp.zeros((nwell, 1), jnp.float32)
    for k in range(caps):
        line = jnp.sum(jnp.where(row_mine, press[k], 0.0), axis=0, keepdims=True)
        hit = jnp.where(own_well == wells[k : k + 1], weights[k : k + 1], 0.0)
        w_sum += jnp.sum(hit, axis=1, keepdims=True)
        p_sum += jnp.sum(hit * line, axis=1, keepdims=True)
    square = lax.broadcasted_iota(jnp.int32, (nwell, nwell), 0) == lax.broadcasted_iota(
        jnp.int32, (nwell, nwell), 1
    )

    def as_row(column):
        return jnp.sum(jnp.where(square, column, 0.0), axis=0, keepdims=True)

    bottom_ref[...] = (rates_ref[...] + as_row(p_sum)) / as_row(w_sum)

    loads[4].wait()

    def blocks(span, r0, r1, r2):
        return [
            inv[i, 0, span] * r0 + inv[i, 1, span] * r1 + inv[i, 2, span] * r2 for i in range(3)
        ]

    for c in range(CHUNKS):
        span = pl.ds(c * rows, rows)
        for side in range(2):

            @pl.when(near[side])
            def _(side=side, c=c):
                for copy in bulk_copies(1 - side, c):
                    copy.wait_recv()

        p, f1, f2 = u[0, span], frac[0, span], frac[1, span]
        q = source[0, span]
        q1, q2 = q * f1, q * f2
        r0 = part[0, span] - (q - q1 - q2)
        r1 = part[1, span] - q1
        r2 = part[2, span] - q2
        for side in range(2):
            h1, h2 = fractions(halo_u[side, 1, span], halo_u[side, 2, span])
            trans = transmissibility(perm[span], halo_k[side, span])
            total = trans * (p - halo_u[side, 0, span])
            s1, s2 = 0.5 * (f1 + h1), 0.5 * (f2 + h2)
            edge[side, 0, span] = trans
            edge[side, 1, span] = 0.5 * total
            edge[side, 2, span] = s1
            edge[side, 3, span] = s2
            flow1, flow2 = total * s1, total * s2
            r0 += total - flow1 - flow2
            r1 += flow1
            r2 += flow2
        res_ref[0, 0, span] = r0
        res_ref[1, 0, span] = r1
        res_ref[2, 0, span] = r2
        d0, d1, d2 = blocks(span, -r0, -r1, -r2)
        g1, g2 = slope[0, span] * d1, slope[1, span] * d2
        mean = f1 * g1 + f2 * g2
        send_d[0, span] = d0
        send_d[1, span] = f1 * (g1 - mean)
        send_d[2, span] = f2 * (g2 - mean)
        corr[0, span] = d1
        corr[1, span] = d2
        for side in range(2):

            @pl.when(near[side])
            def _(side=side, c=c):
                tangent_copy(side, c).start()

    message_d[...] = jnp.zeros_like(message_d)
    for k in range(caps):
        message_d[k : k + 1, :n] = pick(send_d[0], k)
    inbox_d[me] = message_d[...]

    @pl.loop(1, n)
    def _(step):
        well_copy(message_d, inbox_d, welld_send, welld_recv, step).start()

    dp, df1, df2 = send_d[0], send_d[1], send_d[2]
    q = source[0]
    w1, w2 = q * df1, q * df2
    part[0] = res_ref[0, 0] + accum[0] * dp + (w1 + w2)
    part[1] = res_ref[1, 0] + accum[1] * corr[0] - w1
    part[2] = res_ref[2, 0] + accum[2] * corr[1] - w2
    for axis, size in ((0, ny), (1, nz)):
        total = face[axis, 0] * (dp - pltpu.roll(dp, size - 1, axis))
        flow1 = total * face[axis, 2] + face[axis, 1] * (df1 + pltpu.roll(df1, size - 1, axis))
        flow2 = total * face[axis, 3] + face[axis, 1] * (df2 + pltpu.roll(df2, size - 1, axis))
        flow0 = total - flow1 - flow2
        for i, flow in enumerate((flow0, flow1, flow2)):
            part[i] += flow - pltpu.roll(flow, 1, axis)

    @pl.loop(1, n)
    def _(step):
        well_arrival(message_d, inbox_d, welld_send, welld_recv, step).wait_recv()

    press = [turned(inbox_d[:, k, :n]) for k in range(caps)]
    flows = []
    for k in range(caps):
        lift = sum(jnp.sum(t * b, axis=1, keepdims=True) for t, b in zip(shares[k], press))
        flows.append(my_weight[k] * (lift - own(press[k])))
    source[1] = spread(flows)

    for c in range(CHUNKS):
        span = pl.ds(c * rows, rows)
        for side in range(2):

            @pl.when(near[side])
            def _(side=side, c=c):
                tangent_copy(1 - side, c).wait_recv()

        dp, df1, df2 = send_d[0, span], send_d[1, span], send_d[2, span]
        f1, f2 = frac[0, span], frac[1, span]
        q = source[1, span]
        q1, q2 = q * f1, q * f2
        r0 = part[0, span] - (q - q1 - q2)
        r1 = part[1, span] - q1
        r2 = part[2, span] - q2
        for side in range(2):
            total = edge[side, 0, span] * (dp - halo_d[side, 0, span])
            half = edge[side, 1, span]
            flow1 = total * edge[side, 2, span] + half * (df1 + halo_d[side, 1, span])
            flow2 = total * edge[side, 3, span] + half * (df2 + halo_d[side, 2, span])
            r0 += total - flow1 - flow2
            r1 += flow1
            r2 += flow2
        e0, e1, e2 = blocks(span, -r0, -r1, -r2)
        new_ref[0, 0, span] = u[0, span] + (dp + e0)
        new_ref[1, 0, span] = u[1, span] + (corr[0, span] + e1)
        new_ref[2, 0, span] = u[2, span] + (corr[1, span] + e2)

    for c in range(CHUNKS):
        for side in range(2):

            @pl.when(near[side])
            def _(side=side, c=c):
                for copy in bulk_copies(side, c):
                    copy.wait_send()
                tangent_copy(side, c).wait_send()

    @pl.loop(1, n)
    def _(step):
        well_copy(message, inbox, well_send, well_recv, step).wait_send()
        well_copy(message_d, inbox_d, welld_send, welld_recv, step).wait_send()


def shards(
    state,
    old_state,
    pore_volume,
    permeability,
    inverse_blocks,
    perf_cells,
    perf_wells,
    well_index,
    well_rates,
):
    n = lax.axis_size("gx")
    ny, nz = state.shape[2:]
    caps = perf_cells.shape[0]
    lines = -(-(3 * caps + 1) // 8) * 8
    width = -(-max(n, well_rates.shape[0]) // 128) * 128
    any_spec = pl.BlockSpec(memory_space=pl.ANY)
    vmem_spec = pl.BlockSpec(memory_space=pltpu.VMEM)

    def planes(*lead):
        return pltpu.VMEM((*lead, ny, nz), jnp.float32)

    dma = pltpu.SemaphoreType.DMA
    new_state, residual, bottom = pl.pallas_call(
        functools.partial(kernel, n),
        out_shape=(
            jax.ShapeDtypeStruct(state.shape, jnp.float32),
            jax.ShapeDtypeStruct(state.shape, jnp.float32),
            jax.ShapeDtypeStruct((1, well_rates.shape[0]), jnp.float32),
        ),
        in_specs=[any_spec] * 5 + [vmem_spec] * 4,
        out_specs=(vmem_spec, vmem_spec, vmem_spec),
        scratch_shapes=[
            planes(3),
            planes(3),
            planes(),
            planes(),
            planes(3, 3),
            planes(2, 3),
            planes(2),
            planes(2, 3),
            planes(3),
            planes(2),
            planes(2),
            planes(2),
            planes(3),
            planes(2, 4),
            planes(2, 4),
            planes(3),
            planes(2),
            pltpu.VMEM((lines, width), jnp.float32),
            pltpu.VMEM((n, lines, width), jnp.float32),
            pltpu.VMEM((caps, width), jnp.float32),
            pltpu.VMEM((n, caps, width), jnp.float32),
            dma((5,)),
            dma((n,)),
            dma((n,)),
            dma((n,)),
            dma((n,)),
            dma((2, CHUNKS, 2)),
            dma((2, CHUNKS, 2)),
            dma((2, CHUNKS)),
            dma((2, CHUNKS)),
        ],
        compiler_params=pltpu.CompilerParams(
            collective_id=0, has_side_effects=True, vmem_limit_bytes=40 * 1024 * 1024
        ),
    )(
        state,
        old_state,
        pore_volume,
        permeability,
        inverse_blocks,
        perf_cells,
        perf_wells,
        well_index,
        well_rates.reshape(1, -1),
    )
    return new_state, residual, bottom.reshape(-1)


def solution(mesh):
    return jax.shard_map(
        shards,
        mesh=mesh,
        in_specs=(
            P(None, ("groups", "gx"), None, None),
            P(None, ("groups", "gx"), None, None),
            P(("groups", "gx"), None, None),
            P(("groups", "gx"), None, None),
            P(None, None, ("groups", "gx"), None, None),
            P(None, ("groups", "gx")),
            P(None, ("groups", "gx")),
            P(None, ("groups", "gx")),
            P(("groups", "gx")),
        ),
        out_specs=(
            P(None, ("groups", "gx"), None, None),
            P(None, ("groups", "gx"), None, None),
            P(("groups", "gx")),
        ),
        check_vma=False,
    )
```

time: 151 us -> 42.1 us (0.28)
  local copies, waits for them, and re-layouts: 67 us -> 9.76 us
  other arithmetic: 33.9 us -> 0 us
  Pallas kernels: 0 us -> 31.3 us
  starting transfers between devices: 24.4 us -> 0 us
  blocking collectives: 11.5 us -> 0 us
  waiting for transfers between devices: 11.5 us -> 0 us
    pallas_call x0 -> x1, Pallas kernels: none -> 31.3 us  [shards(): pl.pallas_call(functools.partial(kernel, n), out_shape=(jax.ShapeDtypeStr...]
    reshape x2 -> x0, local copies, waits for them, and re-layouts: 20.6 us -> none  [spread(): return placed.reshape(state.shape)]
    all_to_all x3 -> x0, starting transfers between devices: 16.6 us -> none  [the longest x2 11.5 us: deliver(): return lax.all_to_all(blocks, 'gx', split_axis=2, concat_axis=2, tiled=True)]
    gather x4 -> x0, local copies, waits for them, and re-layouts: 15.3 us -> none  [the longest x2 8.38 us: shards(): received_v = deliver(correction.reshape(3, cells)[:, safe])]
    scatter-add x2 -> x0, other arithmetic: 15.2 us -> none  [spread(): jnp.zeros((3, cells), state.dtype).at[:, safe].add(values * mask[None])]
    all_to_all x3 -> x0, waiting for transfers between devices: 11.5 us -> none  [the longest x1 6.37 us: collect(): lax.all_to_all(sources, 'gx', split_axis=2, concat_axis=2, tiled=True)]
    all_to_all x1 -> x0, blocking collectives: 11.5 us -> none  [collect(): lax.all_to_all(sources, 'gx', split_axis=2, concat_axis=2, tiled=True)]
    mul x15 -> x0, other arithmetic: 9.44 us -> none  [the longest x2 2.88 us: apply_blocks(): return jnp.sum(blocks * values[None], axis=1)]
  transfers between devices with their start and end apart: 7 -> 0, of which waited for: 3 -> 0; matrix products, arithmetic and copies ran while one was open for 35% -> 0% of each run, Pallas kernels for 0% -> 0%
where the time goes in v1:
time: 42.1 us; the launch traced here: 41.7 us
  Pallas kernels  31.3 us (74%)
  local copies, waits for them, and re-layouts  9.76 us (23%)
  between operations  0.66 us (2%)
    pallas_call x1, Pallas kernels, shards(): pl.pallas_call(functools.partial(kernel, n), out_shape=(jax.ShapeDtypeStr...  31.3 us
    unnamed x21, local copies, waits for them, and re-layouts  9.76 us

profile of v1, /device:TPU:0, one launch (start us, length us, event | category | flops | bytes accessed | tf_op | source)
XLA Modules:
  0.0 41.7 jit_solution(2018104380134804577)
XLA Ops:
  0.6 0.0 copy-start
  0.6 1.3 %copy-done = f32[3,3,1,128,256]{4,3,2,1,0:T(8,128)S(1)} copy-done((f32[3,3,1,128,256]{4,3,2,1,0:T(8,128)S(1)}, f32[3,3,1,128,256]{4,3,2,1,0:T(8,128)}, u32[]{:S(2)}) %copy-start) | copy-done | bytes 1179672
  1.9 0.0 copy-start.1
  1.9 1.0 %copy-done.1 = f32[3,1,128,256]{3,2,1,0:T(8,128)S(1)} copy-done((f32[3,1,128,256]{3,2,1,0:T(8,128)S(1)}, f32[3,1,128,256]{3,2,1,0:T(8,128)}, u32[]{:S(2)}) %copy-start.1) | copy-done | bytes 393240
  2.9 0.0 copy-start.2
  2.9 1.0 %copy-done.2 = f32[3,1,128,256]{3,2,1,0:T(8,128)S(1)} copy-done((f32[3,1,128,256]{3,2,1,0:T(8,128)S(1)}, f32[3,1,128,256]{3,2,1,0:T(8,128)}, u32[]{:S(2)}) %copy-start.2) | copy-done | bytes 393240
  3.9 0.0 copy-start.3
  3.9 0.9 %copy-done.3 = f32[1,128,256]{2,1,0:T(8,128)S(1)} copy-done((f32[1,128,256]{2,1,0:T(8,128)S(1)}, f32[1,128,256]{2,1,0:T(8,128)}, u32[]{:S(2)}) %copy-start.3) | copy-done | bytes 131096
  4.8 0.0 copy-start.4
  4.8 0.9 %copy-done.4 = f32[1,128,256]{2,1,0:T(8,128)S(1)} copy-done((f32[1,128,256]{2,1,0:T(8,128)S(1)}, f32[1,128,256]{2,1,0:T(8,128)}, u32[]{:S(2)}) %copy-start.4) | copy-done | bytes 131096
  5.7 0.0 copy-start.5
  5.7 0.7 %copy-done.5 = s32[2,16]{1,0:T(2,128)S(1)} copy-done((s32[2,16]{1,0:T(2,128)S(1)}, s32[2,16]{1,0:T(2,128)}, u32[]{:S(2)}) %copy-start.5) | copy-done | bytes 152
  6.4 0.0 copy-start.6
  6.4 0.7 %copy-done.6 = s32[2,16]{1,0:T(2,128)S(1)} copy-done((s32[2,16]{1,0:T(2,128)S(1)}, s32[2,16]{1,0:T(2,128)}, u32[]{:S(2)}) %copy-start.6) | copy-done | bytes 152
  7.1 0.0 copy-start.7
  7.1 0.7 %copy-done.7 = f32[2,16]{1,0:T(2,128)S(1)} copy-done((f32[2,16]{1,0:T(2,128)S(1)}, f32[2,16]{1,0:T(2,128)}, u32[]{:S(2)}) %copy-start.7) | copy-done | bytes 152
  7.7 0.0 copy-start.8
  7.7 0.7 %copy-done.8 = f32[16]{0:T(128)S(1)} copy-done((f32[16]{0:T(128)S(1)}, f32[16]{0:T(128)}, u32[]{:S(2)}) %copy-start.8) | copy-done | bytes 88
  8.4 31.3 %shard_map.112 = (f32[3,1,128,256]{3,2,1,0:T(8,128)S(1)}, f32[3,1,128,256]{3,2,1,0:T(8,128)S(1)}, f32[1,16]{1,0:T(1,128)S(1)}) custom-call(f32[3,1,128,256]{3,2,1,0:T(8,128)S(1)} %copy-done.1, f32[3,1,128,256]{3,2,1,0:T(8,128)S(1)} %copy-done.2, f32[1,128,256]{2,1,0:T(8,128)S(1)} %copy-done.3, f32[1,128,256]{2,1,0:T(8,128)S(1)} %copy-done.4, ...), custom_call_target="tpu_custom_call" | custom-call | tf_op jit(solution)/shard_map/pallas_call | solution.py:453
  39.7 0.7 %copy.15 = f32[3,1,128,256]{3,2,1,0:T(8,128)} copy(f32[3,1,128,256]{3,2,1,0:T(8,128)S(1)} %get-tuple-element.12) | data formatting | bytes 786432
  40.5 0.7 %copy.16 = f32[3,1,128,256]{3,2,1,0:T(8,128)} copy(f32[3,1,128,256]{3,2,1,0:T(8,128)S(1)} %get-tuple-element.13) | data formatting | bytes 786432
  41.2 0.5 %copy.17 = f32[16]{0:T(128)} copy(f32[16]{0:T(128)S(1)} %bitcast.3) | data formatting | bytes 128
Async XLA Ops:
  0.6 1.3 %copy-start = (f32[3,3,1,128,256]{4,3,2,1,0:T(8,128)S(1)}, f32[3,3,1,128,256]{4,3,2,1,0:T(8,128)}, u32[]{:S(2)}) copy-start(f32[3,3,1,128,256]{4,3,2,1,0:T(8,128)} %inv_hbm.1) | copy-start | bytes 3538948
  1.9 1.0 %copy-start.1 = (f32[3,1,128,256]{3,2,1,0:T(8,128)S(1)}, f32[3,1,128,256]{3,2,1,0:T(8,128)}, u32[]{:S(2)}) copy-start(f32[3,1,128,256]{3,2,1,0:T(8,128)} %state_hbm.1) | copy-start | bytes 1179652
  2.9 1.0 %copy-start.2 = (f32[3,1,128,256]{3,2,1,0:T(8,128)S(1)}, f32[3,1,128,256]{3,2,1,0:T(8,128)}, u32[]{:S(2)}) copy-start(f32[3,1,128,256]{3,2,1,0:T(8,128)} %old_hbm.1) | copy-start | bytes 1179652
  3.9 0.9 %copy-start.3 = (f32[1,128,256]{2,1,0:T(8,128)S(1)}, f32[1,128,256]{2,1,0:T(8,128)}, u32[]{:S(2)}) copy-start(f32[1,128,256]{2,1,0:T(8,128)} %pore_hbm.1) | copy-start | bytes 393220
  4.8 0.9 %copy-start.4 = (f32[1,128,256]{2,1,0:T(8,128)S(1)}, f32[1,128,256]{2,1,0:T(8,128)}, u32[]{:S(2)}) copy-start(f32[1,128,256]{2,1,0:T(8,128)} %perm_hbm.1) | copy-start | bytes 393220
  5.7 0.7 %copy-start.5 = (s32[2,16]{1,0:T(2,128)S(1)}, s32[2,16]{1,0:T(2,128)}, u32[]{:S(2)}) copy-start(s32[2,16]{1,0:T(2,128)} %cells_ref.1) | copy-start | bytes 388
  6.4 0.7 %copy-start.6 = (s32[2,16]{1,0:T(2,128)S(1)}, s32[2,16]{1,0:T(2,128)}, u32[]{:S(2)}) copy-start(s32[2,16]{1,0:T(2,128)} %wells_ref.1) | copy-start | bytes 388
  7.1 0.7 %copy-start.7 = (f32[2,16]{1,0:T(2,128)S(1)}, f32[2,16]{1,0:T(2,128)}, u32[]{:S(2)}) copy-start(f32[2,16]{1,0:T(2,128)} %index_ref.1) | copy-start | bytes 388
  7.7 0.7 %copy-start.8 = (f32[16]{0:T(128)S(1)}, f32[16]{0:T(128)}, u32[]{:S(2)}) copy-start(f32[16]{0:T(128)} %param.17) | copy-start | bytes 196

commit v2 on v1

--- a/solution.py
+++ b/solution.py
@@ -8,6 +8,7 @@
 from jax.sharding import PartitionSpec as P
 
 CHUNKS = 4
+VMEM_LIMIT = 62 * 1024 * 1024
 MESH = pl.DeviceIdType.MESH
 EXACT = lax.Precision.HIGHEST
 
@@ -40,18 +41,26 @@
     pore_hbm,
     perm_hbm,
     inv_hbm,
-    cells_ref,
-    wells_ref,
-    index_ref,
-    rates_ref,
+    cells_hbm,
+    wells_hbm,
+    index_hbm,
+    rates_hbm,
+    new_hbm,
+    res_hbm,
+    bottom_hbm,
     new_ref,
     res_ref,
     bottom_ref,
+    save_sem,
     u,
     old,
     pore,
     perm,
     inv,
+    cells_ref,
+    wells_ref,
+    index_ref,
+    rates_ref,
     halo_u,
     halo_k,
     halo_d,
@@ -90,9 +99,22 @@
         pltpu.make_async_copy(old_hbm.at[:, 0], old, load_sem.at[2]),
         pltpu.make_async_copy(pore_hbm.at[0], pore, load_sem.at[3]),
         pltpu.make_async_copy(inv_hbm.at[:, :, 0], inv, load_sem.at[4]),
+        pltpu.make_async_copy(cells_hbm, cells_ref, load_sem.at[5]),
+        pltpu.make_async_copy(wells_hbm, wells_ref, load_sem.at[6]),
+        pltpu.make_async_copy(index_hbm, index_ref, load_sem.at[7]),
+        pltpu.make_async_copy(rates_hbm, rates_ref, load_sem.at[8]),
     ]
-    for load in loads:
+    for load in loads[5:] + loads[:5]:
         load.start()
+
+    saves = [pltpu.make_async_copy(bottom_ref, bottom_hbm, save_sem.at[2 * CHUNKS])]
+
+    def save(source_ref, target_ref, span, slot):
+        copy = pltpu.make_async_copy(
+            source_ref.at[:, :, span], target_ref.at[:, :, span], save_sem.at[slot]
+        )
+        copy.start()
+        saves.append(copy)
 
     barrier = pltpu.get_barrier_semaphore()
 
@@ -102,6 +124,8 @@
             barrier, inc=1, device_id={"gx": lax.rem(me + step, n)}, device_id_type=MESH
         )
 
+    for load in loads[5:]:
+        load.wait()
     cells = cells_ref[...]
     cell_y = cells // nz
     cell_z = cells - cell_y * nz
@@ -297,6 +321,7 @@
         return jnp.sum(jnp.where(square, column, 0.0), axis=0, keepdims=True)
 
     bottom_ref[...] = (rates_ref[...] + as_row(p_sum)) / as_row(w_sum)
+    saves[0].start()
 
     loads[4].wait()
 
@@ -336,6 +361,7 @@
         res_ref[0, 0, span] = r0
         res_ref[1, 0, span] = r1
         res_ref[2, 0, span] = r2
+        save(res_ref, res_hbm, span, c)
         d0, d1, d2 = blocks(span, -r0, -r1, -r2)
         g1, g2 = slope[0, span] * d1, slope[1, span] * d2
         mean = f1 * g1 + f2 * g2
@@ -411,6 +437,10 @@
         new_ref[0, 0, span] = u[0, span] + (dp + e0)
         new_ref[1, 0, span] = u[1, span] + (corr[0, span] + e1)
         new_ref[2, 0, span] = u[2, span] + (corr[1, span] + e2)
+        save(new_ref, new_hbm, span, CHUNKS + c)
+
+    for copy in saves:
+        copy.wait()
 
     for c in range(CHUNKS):
         for side in range(2):
@@ -425,6 +455,16 @@
     def _(step):
         well_copy(message, inbox, well_send, well_recv, step).wait_send()
         well_copy(message_d, inbox_d, welld_send, welld_recv, step).wait_send()
+
+
+def store(*refs):
+    copies = [
+        pltpu.make_async_copy(refs[i], refs[3 + i], refs[6].at[i]) for i in range(3)
+    ]
+    for copy in copies:
+        copy.start()
+    for copy in copies:
+        copy.wait()
 
 
 def shards(
@@ -443,28 +483,36 @@
     caps = perf_cells.shape[0]
     lines = -(-(3 * caps + 1) // 8) * 8
     width = -(-max(n, well_rates.shape[0]) // 128) * 128
-    any_spec = pl.BlockSpec(memory_space=pl.ANY)
-    vmem_spec = pl.BlockSpec(memory_space=pltpu.VMEM)
+    hbm_spec = pl.BlockSpec(memory_space=pltpu.HBM)
 
     def planes(*lead):
         return pltpu.VMEM((*lead, ny, nz), jnp.float32)
 
     dma = pltpu.SemaphoreType.DMA
-    new_state, residual, bottom = pl.pallas_call(
+    out_shape = (
+        jax.ShapeDtypeStruct(state.shape, jnp.float32),
+        jax.ShapeDtypeStruct(state.shape, jnp.float32),
+        jax.ShapeDtypeStruct((1, well_rates.shape[0]), jnp.float32),
+    )
+    results = pl.pallas_call(
         functools.partial(kernel, n),
-        out_shape=(
-            jax.ShapeDtypeStruct(state.shape, jnp.float32),
-            jax.ShapeDtypeStruct(state.shape, jnp.float32),
-            jax.ShapeDtypeStruct((1, well_rates.shape[0]), jnp.float32),
-        ),
-        in_specs=[any_spec] * 5 + [vmem_spec] * 4,
-        out_specs=(vmem_spec, vmem_spec, vmem_spec),
+        out_shape=out_shape,
+        in_specs=[hbm_spec] * 9,
+        out_specs=(hbm_spec,) * 3,
         scratch_shapes=[
+            planes(3, 1),
+            planes(3, 1),
+            pltpu.VMEM((1, well_rates.shape[0]), jnp.float32),
+            dma((2 * CHUNKS + 1,)),
             planes(3),
             planes(3),
             planes(),
             planes(),
             planes(3, 3),
+            pltpu.VMEM(perf_cells.shape, jnp.int32),
+            pltpu.VMEM(perf_wells.shape, jnp.int32),
+            pltpu.VMEM(well_index.shape, jnp.float32),
+            pltpu.VMEM((1, well_rates.shape[0]), jnp.float32),
             planes(2, 3),
             planes(2),
             planes(2, 3),
@@ -481,7 +529,7 @@
             pltpu.VMEM((n, lines, width), jnp.float32),
             pltpu.VMEM((caps, width), jnp.float32),
             pltpu.VMEM((n, caps, width), jnp.float32),
-            dma((5,)),
+            dma((9,)),
             dma((n,)),
             dma((n,)),
             dma((n,)),
@@ -492,7 +540,7 @@
             dma((2, CHUNKS)),
         ],
         compiler_params=pltpu.CompilerParams(
-            collective_id=0, has_side_effects=True, vmem_limit_bytes=40 * 1024 * 1024
+            collective_id=0, has_side_effects=True, vmem_limit_bytes=VMEM_LIMIT
         ),
     )(
         state,
@@ -505,6 +553,14 @@
         well_index,
         well_rates.reshape(1, -1),
     )
+    new_state, residual, bottom = pl.pallas_call(
+        store,
+        out_shape=out_shape,
+        in_specs=[pl.BlockSpec(memory_space=pl.ANY)] * 3,
+        out_specs=(hbm_spec,) * 3,
+        scratch_shapes=[dma((3,))],
+        compiler_params=pltpu.CompilerParams(vmem_limit_bytes=VMEM_LIMIT),
+    )(*results)
     return new_state, residual, bottom.reshape(-1)
 
 

time: 42.1 us -> 56.9 us (1.35)
  Pallas kernels: 31.3 us -> 56.1 us
  local copies, waits for them, and re-layouts: 9.76 us -> 0 us
    pallas_call x1 -> x2, Pallas kernels: 31.3 us -> 56.1 us  [the longest x1 31.1 us: shards(): pl.pallas_call(functools.partial(kernel, n), out_shape=out_shape, in_spec...]
    unnamed x21 -> x0, local copies, waits for them, and re-layouts: 9.76 us -> none
where the time goes in v2:
time: 56.9 us; the launch traced here: 56.8 us
  Pallas kernels  56.1 us (99%)
  between operations  0.64 us (1%)
    pallas_call x1, Pallas kernels, shards(): pl.pallas_call(functools.partial(kernel, n), out_shape=out_shape, in_spec...  31.1 us
    pallas_call x1, Pallas kernels, shards(): pl.pallas_call(store, out_shape=out_shape, in_specs=[pl.BlockSpec(memory_...  25 us

profile of v2, /device:TPU:0, one launch (start us, length us, event | category | flops | bytes accessed | tf_op | source)
XLA Modules:
  0.0 56.8 jit_solution(2323814735158822914)
XLA Ops:
  0.6 31.1 %shard_map.112 = (f32[3,1,128,256]{3,2,1,0:T(8,128)}, f32[3,1,128,256]{3,2,1,0:T(8,128)}, f32[1,16]{1,0:T(1,128)}) custom-call(f32[3,1,128,256]{3,2,1,0:T(8,128)} %state_hbm.1, f32[3,1,128,256]{3,2,1,0:T(8,128)} %old_hbm.1, f32[1,128,256]{2,1,0:T(8,128)} %pore_hbm.1, f32[1,128,256]{2,1,0:T(8,128)} %perm_hbm.1, f32[3,3,1,128,256]{4,3,2,1,0:T(8,128)} %inv_hbm.1, ...), custom_call_target="tpu_custom_call" | custom-call | tf_op jit(solution)/shard_map/pallas_call | solution.py:497
  31.8 25.0 %shard_map.113 = (f32[3,1,128,256]{3,2,1,0:T(8,128)}, f32[3,1,128,256]{3,2,1,0:T(8,128)}, f32[1,16]{1,0:T(1,128)}) custom-call(f32[3,1,128,256]{3,2,1,0:T(8,128)} %get-tuple-element.9.refs_0_, f32[3,1,128,256]{3,2,1,0:T(8,128)} %get-tuple-element.10.refs_1_, f32[1,16]{1,0:T(1,128)} %get-tuple-element.11.refs_2_), custom_call_target="tpu_custom_call" | custom-call | tf_op jit(solution)/shard_map/pallas_call | solution.py:556

commit v3 on v2

--- a/solution.py
+++ b/solution.py
@@ -458,13 +458,16 @@
 
 
 def store(*refs):
-    copies = [
-        pltpu.make_async_copy(refs[i], refs[3 + i], refs[6].at[i]) for i in range(3)
-    ]
-    for copy in copies:
-        copy.start()
-    for copy in copies:
-        copy.wait()
+    ins, outs, held, load_sem, save_sem = refs[:3], refs[3:6], refs[6:9], refs[9], refs[10]
+    loads = [pltpu.make_async_copy(ins[i], held[i], load_sem.at[i]) for i in range(3)]
+    saves = [pltpu.make_async_copy(held[i], outs[i], save_sem.at[i]) for i in range(3)]
+    for load in loads:
+        load.start()
+    for load, save in zip(loads, saves):
+        load.wait()
+        save.start()
+    for save in saves:
+        save.wait()
 
 
 def shards(
@@ -558,7 +561,8 @@
         out_shape=out_shape,
         in_specs=[pl.BlockSpec(memory_space=pl.ANY)] * 3,
         out_specs=(hbm_spec,) * 3,
-        scratch_shapes=[dma((3,))],
+        scratch_shapes=[pltpu.VMEM(shape.shape, shape.dtype) for shape in out_shape]
+        + [dma((3,)), dma((3,))],
         compiler_params=pltpu.CompilerParams(vmem_limit_bytes=VMEM_LIMIT),
     )(*results)
     return new_state, residual, bottom.reshape(-1)

time: 56.9 us -> 33.9 us (0.60)
  Pallas kernels: 56.1 us -> 33.1 us
    pallas_call x1, Pallas kernels: 25 us -> 1.92 us  [shards(): pl.pallas_call(store, out_shape=out_shape, in_specs=[pl.BlockSpec(memory_...]
where the time goes in v3:
time: 33.9 us; the launch traced here: 33.7 us
  Pallas kernels  33.1 us (98%)
  between operations  0.64 us (2%)
    pallas_call x1, Pallas kernels, shards(): pl.pallas_call(functools.partial(kernel, n), out_shape=out_shape, in_spec...  31.1 us
    pallas_call x1, Pallas kernels, shards(): pl.pallas_call(store, out_shape=out_shape, in_specs=[pl.BlockSpec(memory_...  1.92 us

profile of v3, /device:TPU:0, one launch (start us, length us, event | category | flops | bytes accessed | tf_op | source)
XLA Modules:
  0.0 33.7 jit_solution(7534148600428702371)
XLA Ops:
  0.6 31.1 %shard_map.112 = (f32[3,1,128,256]{3,2,1,0:T(8,128)}, f32[3,1,128,256]{3,2,1,0:T(8,128)}, f32[1,16]{1,0:T(1,128)}) custom-call(f32[3,1,128,256]{3,2,1,0:T(8,128)} %state_hbm.1, f32[3,1,128,256]{3,2,1,0:T(8,128)} %old_hbm.1, f32[1,128,256]{2,1,0:T(8,128)} %pore_hbm.1, f32[1,128,256]{2,1,0:T(8,128)} %perm_hbm.1, f32[3,3,1,128,256]{4,3,2,1,0:T(8,128)} %inv_hbm.1, ...), custom_call_target="tpu_custom_call" | custom-call | tf_op jit(solution)/shard_map/pallas_call | solution.py:500
  31.8 1.9 %shard_map.113 = (f32[3,1,128,256]{3,2,1,0:T(8,128)}, f32[3,1,128,256]{3,2,1,0:T(8,128)}, f32[1,16]{1,0:T(1,128)}) custom-call(f32[3,1,128,256]{3,2,1,0:T(8,128)} %get-tuple-element.9.refs_0_, f32[3,1,128,256]{3,2,1,0:T(8,128)} %get-tuple-element.10.refs_1_, f32[1,16]{1,0:T(1,128)} %get-tuple-element.11.refs_2_), custom_call_target="tpu_custom_call" | custom-call | tf_op jit(solution)/shard_map/pallas_call | solution.py:559

commit v4 on v3

--- a/solution.py
+++ b/solution.py
@@ -141,15 +141,27 @@
     def pick(plane, k):
         return jnp.sum(contract(plane, at_z[k], 1, 0) * at_y[k], axis=0, keepdims=True)
 
+    each = message.shape[1] // max(n, nwell)
+    stride = message.shape[1] // each
+
+    def seat(piece, size):
+        line, first = piece // each, piece % each * stride
+        return pl.ds(line, 1), pl.ds(first, size)
+
+    def piece_of(box, piece, size):
+        line, first = piece // each, piece % each * stride
+        return box[:, line, first : first + size]
+
     wells = wells_ref[...]
     weights = jnp.where(wells >= 0, index_ref[...], 0.0)
     message[...] = jnp.zeros_like(message)
-    message[caps : 2 * caps, :n] = weights
-    message[2 * caps : 3 * caps, :n] = wells.astype(jnp.float32)
-    message[3 * caps : 3 * caps + 1, :nwell] = rates_ref[...]
+    for k in range(caps):
+        message[seat(caps + k, n)] = weights[k : k + 1]
+        message[seat(2 * caps + k, n)] = wells[k : k + 1].astype(jnp.float32)
+    message[seat(3 * caps, nwell)] = rates_ref[...]
     loads[0].wait()
     for k in range(caps):
-        message[k : k + 1, :n] = pick(u[0], k)
+        message[seat(k, n)] = pick(u[0], k)
     inbox[me] = message[...]
     loads[1].wait()
 
@@ -275,10 +287,10 @@
     def own(values):
         return jnp.sum(jnp.where(mine, values, 0.0), axis=1, keepdims=True)
 
-    press = [turned(inbox[:, k, :n]) for k in range(caps)]
-    weight = [inbox[:, caps + k, :n] for k in range(caps)]
-    well = [inbox[:, 2 * caps + k, :n] for k in range(caps)]
-    rates = inbox[:, 3 * caps, :nwell]
+    press = [turned(piece_of(inbox, k, n)) for k in range(caps)]
+    weight = [piece_of(inbox, caps + k, n) for k in range(caps)]
+    well = [piece_of(inbox, 2 * caps + k, n) for k in range(caps)]
+    rates = piece_of(inbox, 3 * caps, nwell)
     well_lane = lax.broadcasted_iota(jnp.int32, (n, nwell), 1).astype(jnp.float32)
     my_weight, shares, flows = [], [], []
     for k in range(caps):
@@ -378,7 +390,7 @@
 
     message_d[...] = jnp.zeros_like(message_d)
     for k in range(caps):
-        message_d[k : k + 1, :n] = pick(send_d[0], k)
+        message_d[seat(k, n)] = pick(send_d[0], k)
     inbox_d[me] = message_d[...]
 
     @pl.loop(1, n)
@@ -403,7 +415,7 @@
     def _(step):
         well_arrival(message_d, inbox_d, welld_send, welld_recv, step).wait_recv()
 
-    press = [turned(inbox_d[:, k, :n]) for k in range(caps)]
+    press = [turned(piece_of(inbox_d, k, n)) for k in range(caps)]
     flows = []
     for k in range(caps):
         lift = sum(jnp.sum(t * b, axis=1, keepdims=True) for t, b in zip(shares[k], press))
@@ -459,8 +471,16 @@
 
 def store(*refs):
     ins, outs, held, load_sem, save_sem = refs[:3], refs[3:6], refs[6:9], refs[9], refs[10]
-    loads = [pltpu.make_async_copy(ins[i], held[i], load_sem.at[i]) for i in range(3)]
-    saves = [pltpu.make_async_copy(held[i], outs[i], save_sem.at[i]) for i in range(3)]
+    whole = list(zip(ins, outs, held))
+    pieces = [whole[2]] + [tuple(ref.at[j] for ref in refs3) for refs3 in whole[:2] for j in range(3)]
+    loads = [
+        pltpu.make_async_copy(source, hold, load_sem.at[i])
+        for i, (source, _, hold) in enumerate(pieces)
+    ]
+    saves = [
+        pltpu.make_async_copy(hold, target, save_sem.at[i])
+        for i, (_, target, hold) in enumerate(pieces)
+    ]
     for load in loads:
         load.start()
     for load, save in zip(loads, saves):
@@ -484,8 +504,10 @@
     n = lax.axis_size("gx")
     ny, nz = state.shape[2:]
     caps = perf_cells.shape[0]
-    lines = -(-(3 * caps + 1) // 8) * 8
-    width = -(-max(n, well_rates.shape[0]) // 128) * 128
+    widest = max(n, well_rates.shape[0])
+    width = -(-widest // 128) * 128
+    each = width // widest
+    lines, lines_d = -(-(3 * caps + 1) // each), -(-caps // each)
     hbm_spec = pl.BlockSpec(memory_space=pltpu.HBM)
 
     def planes(*lead):
@@ -530,8 +552,8 @@
             planes(2),
             pltpu.VMEM((lines, width), jnp.float32),
             pltpu.VMEM((n, lines, width), jnp.float32),
-            pltpu.VMEM((caps, width), jnp.float32),
-            pltpu.VMEM((n, caps, width), jnp.float32),
+            pltpu.VMEM((lines_d, width), jnp.float32),
+            pltpu.VMEM((n, lines_d, width), jnp.float32),
             dma((9,)),
             dma((n,)),
             dma((n,)),
@@ -562,7 +584,7 @@
         in_specs=[pl.BlockSpec(memory_space=pl.ANY)] * 3,
         out_specs=(hbm_spec,) * 3,
         scratch_shapes=[pltpu.VMEM(shape.shape, shape.dtype) for shape in out_shape]
-        + [dma((3,)), dma((3,))],
+        + [dma((7,)), dma((7,))],
         compiler_params=pltpu.CompilerParams(vmem_limit_bytes=VMEM_LIMIT),
     )(*results)
     return new_state, residual, bottom.reshape(-1)

time: 33.9 us -> 33.3 us (0.982)
  Pallas kernels: 33.1 us -> 32.5 us
    pallas_call x1, Pallas kernels: 31.1 us -> 30.5 us  [shards(): pl.pallas_call(functools.partial(kernel, n), out_shape=out_shape, in_spec...]
where the time goes in v4:
time: 33.3 us; the launch traced here: 33.1 us
  Pallas kernels  32.5 us (98%)
  between operations  0.64 us (2%)
    pallas_call x1, Pallas kernels, shards(): pl.pallas_call(functools.partial(kernel, n), out_shape=out_shape, in_spec...  30.5 us
    pallas_call x1, Pallas kernels, shards(): pl.pallas_call(store, out_shape=out_shape, in_specs=[pl.BlockSpec(memory_...  1.99 us

profile of v4, /device:TPU:0, one launch (start us, length us, event | category | flops | bytes accessed | tf_op | source)
XLA Modules:
  0.0 33.1 jit_solution(9418235362306940617)
XLA Ops:
  0.6 30.5 %shard_map.112 = (f32[3,1,128,256]{3,2,1,0:T(8,128)}, f32[3,1,128,256]{3,2,1,0:T(8,128)}, f32[1,16]{1,0:T(1,128)}) custom-call(f32[3,1,128,256]{3,2,1,0:T(8,128)} %state_hbm.1, f32[3,1,128,256]{3,2,1,0:T(8,128)} %old_hbm.1, f32[1,128,256]{2,1,0:T(8,128)} %pore_hbm.1, f32[1,128,256]{2,1,0:T(8,128)} %perm_hbm.1, f32[3,3,1,128,256]{4,3,2,1,0:T(8,128)} %inv_hbm.1, ...), custom_call_target="tpu_custom_call" | custom-call | tf_op jit(solution)/shard_map/pallas_call | solution.py:522
  31.1 2.0 %shard_map.113 = (f32[3,1,128,256]{3,2,1,0:T(8,128)}, f32[3,1,128,256]{3,2,1,0:T(8,128)}, f32[1,16]{1,0:T(1,128)}) custom-call(f32[3,1,128,256]{3,2,1,0:T(8,128)} %get-tuple-element.9.refs_0_, f32[3,1,128,256]{3,2,1,0:T(8,128)} %get-tuple-element.10.refs_1_, f32[1,16]{1,0:T(1,128)} %get-tuple-element.11.refs_2_), custom_call_target="tpu_custom_call" | custom-call | tf_op jit(solution)/shard_map/pallas_call | solution.py:581

commit v5 on v4

--- a/solution.py
+++ b/solution.py
@@ -45,13 +45,9 @@
     wells_hbm,
     index_hbm,
     rates_hbm,
-    new_hbm,
-    res_hbm,
-    bottom_hbm,
     new_ref,
     res_ref,
     bottom_ref,
-    save_sem,
     u,
     old,
     pore,
@@ -107,15 +103,6 @@
     for load in loads[5:] + loads[:5]:
         load.start()
 
-    saves = [pltpu.make_async_copy(bottom_ref, bottom_hbm, save_sem.at[2 * CHUNKS])]
-
-    def save(source_ref, target_ref, span, slot):
-        copy = pltpu.make_async_copy(
-            source_ref.at[:, :, span], target_ref.at[:, :, span], save_sem.at[slot]
-        )
-        copy.start()
-        saves.append(copy)
-
     barrier = pltpu.get_barrier_semaphore()
 
     @pl.loop(1, n)
@@ -333,8 +320,6 @@
         return jnp.sum(jnp.where(square, column, 0.0), axis=0, keepdims=True)
 
     bottom_ref[...] = (rates_ref[...] + as_row(p_sum)) / as_row(w_sum)
-    saves[0].start()
-
     loads[4].wait()
 
     def blocks(span, r0, r1, r2):
@@ -373,7 +358,6 @@
         res_ref[0, 0, span] = r0
         res_ref[1, 0, span] = r1
         res_ref[2, 0, span] = r2
-        save(res_ref, res_hbm, span, c)
         d0, d1, d2 = blocks(span, -r0, -r1, -r2)
         g1, g2 = slope[0, span] * d1, slope[1, span] * d2
         mean = f1 * g1 + f2 * g2
@@ -449,10 +433,6 @@
         new_ref[0, 0, span] = u[0, span] + (dp + e0)
         new_ref[1, 0, span] = u[1, span] + (corr[0, span] + e1)
         new_ref[2, 0, span] = u[2, span] + (corr[1, span] + e2)
-        save(new_ref, new_hbm, span, CHUNKS + c)
-
-    for copy in saves:
-        copy.wait()
 
     for c in range(CHUNKS):
         for side in range(2):
@@ -470,24 +450,11 @@
 
 
 def store(*refs):
-    ins, outs, held, load_sem, save_sem = refs[:3], refs[3:6], refs[6:9], refs[9], refs[10]
-    whole = list(zip(ins, outs, held))
-    pieces = [whole[2]] + [tuple(ref.at[j] for ref in refs3) for refs3 in whole[:2] for j in range(3)]
-    loads = [
-        pltpu.make_async_copy(source, hold, load_sem.at[i])
-        for i, (source, _, hold) in enumerate(pieces)
-    ]
-    saves = [
-        pltpu.make_async_copy(hold, target, save_sem.at[i])
-        for i, (_, target, hold) in enumerate(pieces)
-    ]
-    for load in loads:
-        load.start()
-    for load, save in zip(loads, saves):
-        load.wait()
-        save.start()
-    for save in saves:
-        save.wait()
+    copies = [pltpu.make_async_copy(refs[i], refs[3 + i], refs[6].at[i]) for i in range(3)]
+    for copy in copies:
+        copy.start()
+    for copy in copies:
+        copy.wait()
 
 
 def shards(
@@ -521,14 +488,10 @@
     )
     results = pl.pallas_call(
         functools.partial(kernel, n),
-        out_shape=out_shape,
+        out_shape=tuple(pltpu.VMEM(shape.shape, shape.dtype) for shape in out_shape),
         in_specs=[hbm_spec] * 9,
-        out_specs=(hbm_spec,) * 3,
+        out_specs=(pl.BlockSpec(memory_space=pltpu.VMEM),) * 3,
         scratch_shapes=[
-            planes(3, 1),
-            planes(3, 1),
-            pltpu.VMEM((1, well_rates.shape[0]), jnp.float32),
-            dma((2 * CHUNKS + 1,)),
             planes(3),
             planes(3),
             planes(),
@@ -581,11 +544,10 @@
     new_state, residual, bottom = pl.pallas_call(
         store,
         out_shape=out_shape,
-        in_specs=[pl.BlockSpec(memory_space=pl.ANY)] * 3,
+        in_specs=[pl.BlockSpec(memory_space=pltpu.VMEM)] * 3,
         out_specs=(hbm_spec,) * 3,
-        scratch_shapes=[pltpu.VMEM(shape.shape, shape.dtype) for shape in out_shape]
-        + [dma((7,)), dma((7,))],
-        compiler_params=pltpu.CompilerParams(vmem_limit_bytes=VMEM_LIMIT),
+        scratch_shapes=[dma((3,))],
+        compiler_params=pltpu.CompilerParams(vmem_limit_bytes=16 * 1024 * 1024),
     )(*results)
     return new_state, residual, bottom.reshape(-1)
 

time: 33.3 us -> 31.5 us (0.946)
  Pallas kernels: 32.5 us -> 30.7 us
    pallas_call x1, Pallas kernels: 1.99 us -> 0.91 us  [shards(): pl.pallas_call(store, out_shape=out_shape, in_specs=[pl.BlockSpec(memory_...]
    pallas_call x1, Pallas kernels: 30.5 us -> 29.8 us  [shards(): pl.pallas_call(functools.partial(kernel, n), out_shape=tuple((pltpu.VMEM(...]
where the time goes in v5:
time: 31.5 us; the launch traced here: 31.3 us
  Pallas kernels  30.7 us (97%)
  between operations  0.64 us (2%)
    pallas_call x1, Pallas kernels, shards(): pl.pallas_call(functools.partial(kernel, n), out_shape=tuple((pltpu.VMEM(...  29.8 us
    pallas_call x1, Pallas kernels, shards(): pl.pallas_call(store, out_shape=out_shape, in_specs=[pl.BlockSpec(memory_...  0.91 us

profile of v5, /device:TPU:0, one launch (start us, length us, event | category | flops | bytes accessed | tf_op | source)
XLA Modules:
  0.0 31.3 jit_solution(1187539315520908579)
XLA Ops:
  0.6 29.8 %shard_map.112 = (f32[3,1,128,256]{3,2,1,0:T(8,128)S(1)}, f32[3,1,128,256]{3,2,1,0:T(8,128)S(1)}, f32[1,16]{1,0:T(1,128)S(1)}) custom-call(f32[3,1,128,256]{3,2,1,0:T(8,128)} %state_hbm.1, f32[3,1,128,256]{3,2,1,0:T(8,128)} %old_hbm.1, f32[1,128,256]{2,1,0:T(8,128)} %pore_hbm.1, f32[1,128,256]{2,1,0:T(8,128)} %perm_hbm.1, f32[3,3,1,128,256]{4,3,2,1,0:T(8,128)} %inv_hbm.1, ...), custom_call_target="tpu_custom_call" | custom-call | tf_op jit(solution)/shard_map/pallas_call | solution.py:489
  30.4 0.9 %shard_map.113 = (f32[3,1,128,256]{3,2,1,0:T(8,128)}, f32[3,1,128,256]{3,2,1,0:T(8,128)}, f32[1,16]{1,0:T(1,128)}) custom-call(f32[3,1,128,256]{3,2,1,0:T(8,128)S(1)} %get-tuple-element.9.refs_0_, f32[3,1,128,256]{3,2,1,0:T(8,128)S(1)} %get-tuple-element.10.refs_1_, f32[1,16]{1,0:T(1,128)S(1)} %get-tuple-element.11.refs_2_), custom_call_target="tpu_custom_call" | custom-call | tf_op jit(solution)/shard_map/pallas_call | solution.py:544
